TPU v7x, 256 devices: a whole 4x4x8 slice. The times are simulated.
256 devices in a mesh: row: 8 (over z), col: 16 (over x, y), layer: 2 (over core).
Axes of the slice: x: 4, y: 4, z: 8, core: 2. Of those that a mesh axis runs over, the one named last changes fastest.
Arguments:
- coeffs: bfloat16 [16384, 4096], P('row', 'col'), may hold values from -6 to 6
- block_sizes: int32 [128], P('row'), may hold values from 64 to 128, as said below
- neighbours: int32 [128, 16], P('row'), may hold values from 0 to 127, as said below
- ham_blocks: bfloat16 [128, 16, 128, 128], P('row', 'layer'), may hold values from -0.125 to 0.125
- ovl_blocks: bfloat16 [128, 16, 128, 128], P('row', 'layer'), may hold values from -0.125 to 0.125
Outputs:
- residual: float32 [16384, 4096], P(('row', 'layer'), 'col')
Inputs may be any that keep to these rules, and one draw needn't show every extreme that they name: `block_sizes`: some block has exactly 128 live basis functions. `neighbours`: every entry names a block at most 16 blocks from its row's block; slot 0 names the row's own block.
All inputs are finite; a program needn't handle non-finite values.
Results may differ from a plain program's by a relative error of at most 0.0031.
Values may be sent and summed in bfloat16 or wider, within the bound.
A program may use at most 128 MiB of HBM per device.

v0:
```python
import jax
import jax.numpy as jnp
from jax import lax
from jax.sharding import PartitionSpec as P


def padded_2(shard, sides, width):
    for axis, dim in sides:
        devices, length = (lax.axis_size(axis), shard.shape[dim])
        up = [(i, (i + 1) % devices) for i in range(devices - 1)]
        down = [(j, i) for i, j in up]
        last = lax.slice_in_dim(shard, length - width, length, axis=dim)
        first = lax.slice_in_dim(shard, 0, width, axis=dim)
        before = lax.ppermute(last, axis, up)
        after = lax.ppermute(first, axis, down)
        shard = jnp.concatenate([before, shard, after], axis=dim)
    return shard


def body(coeffs, block_sizes, neighbours, ham_blocks, ovl_blocks):
    blocks_dev = block_sizes.shape[0]
    block_rows = ham_blocks.shape[2]
    cols_dev = coeffs.shape[1]
    slots_all = neighbours.shape[1]
    layer_id = lax.axis_index("layer")
    live = jnp.arange(block_rows, dtype=jnp.int32)[None, :] < block_sizes[:, None]
    masked = (
        coeffs.reshape(blocks_dev, block_rows, cols_dev) * live[:, :, None].astype(coeffs.dtype)
    ).reshape(blocks_dev * block_rows, cols_dev)
    padded = padded_2(masked, (("row", 0),), blocks_dev * block_rows)
    padded = padded.reshape(3 * blocks_dev, block_rows, cols_dev)
    first_block = lax.axis_index("row") * blocks_dev - blocks_dev
    live_float = live.astype(jnp.float32)
    half_blocks = blocks_dev // 2
    half_rows = half_blocks * block_rows
    slots_dev = slots_all // 2
    layer_neigh = lax.dynamic_slice_in_dim(neighbours, layer_id * slots_dev, slots_dev, 1)
    picked = padded[layer_neigh - first_block]
    nsel = lax.axis_size("layer") * half_rows // block_rows
    wpart = (
        jnp.einsum("ikpq,ikqn->ipn", ham_blocks, picked, preferred_element_type=jnp.float32)
        * live_float[:, :, None]
    )
    vpart = (
        jnp.einsum("ikpq,ikqn->ipn", ovl_blocks, picked, preferred_element_type=jnp.float32)
        * live_float[:, :, None]
    )
    both = jnp.concatenate([wpart, vpart], axis=2)
    summed = lax.psum_scatter(
        both.reshape(nsel * block_rows, 2 * cols_dev), "layer", scatter_dimension=0, tiled=True
    )
    hc_half = summed[:, :cols_dev].astype(jnp.bfloat16)
    sc_half = summed[:, cols_dev:].astype(jnp.bfloat16)
    masked_half = lax.dynamic_slice_in_dim(masked, layer_id * half_rows, half_rows, 0)
    total_rows = blocks_dev * block_rows * lax.axis_size("row")
    partial_gram = lax.dot_general(
        lax.all_gather(masked_half, "col", axis=1, tiled=True),
        hc_half,
        (((0,), (0,)), ((), ())),
        preferred_element_type=jnp.float32,
    )
    whole_gram = lax.psum(partial_gram, ("row", "layer"))
    gram = (whole_gram / total_rows).astype(jnp.bfloat16)
    projected = jnp.dot(
        lax.all_gather(sc_half, "col", axis=1, tiled=True), gram, preferred_element_type=jnp.float32
    )
    return hc_half.astype(jnp.float32) - projected


def solution(mesh):
    return jax.shard_map(
        body,
        mesh=mesh,
        in_specs=(
            P("row", "col"),
            P("row"),
            P("row", None),
            P("row", "layer", None, None),
            P("row", "layer", None, None),
        ),
        out_specs=P(("row", "layer"), "col"),
        check_vma=False,
    )
```

profile of v0, /device:TPU:1, one launch (start us, length us, event | category | flops | bytes accessed | tf_op | source)
XLA Modules:
  0.0 304.2 jit_solution(10484803726744755979)
XLA Ops:
  7.4 0.0 reduce-scatter.2.cloned.1.call-start
  7.4 0.7 fusion.7
  8.1 1.6 broadcast_multiply_fusion
  9.7 0.0 copy-start
  9.7 4.4 %collective-permute-start = (bf16[2048,256]{1,0:T(8,128)(2,1)S(1)}, bf16[2048,256]{1,0:T(8,128)(2,1)S(1)}, u32[]{:S(2)}, u32[]{:S(2)}) collective-permute-start(bf16[2048,256]{1,0:T(8,128)(2,1)S(1)} %broadcast_multiply_fusion), channel_id=1, source_target_pairs={{0,32},{32,64},{64,96},{96,128},{128,160},{160,192},{192,224},{1,3... | collective-permute-start | bytes 3145736 | tf_op jit(solution)/shard_map/ppermute | solution.py:14
  14.1 1.3 collective-permute-start.1
  15.4 0.8 compare_select_fusion
  16.2 0.1 reshape.56
  16.3 19.6 %collective-permute-done = bf16[2048,256]{1,0:T(8,128)(2,1)S(1)} collective-permute-done((bf16[2048,256]{1,0:T(8,128)(2,1)S(1)}, bf16[2048,256]{1,0:T(8,128)(2,1)S(1)}, u32[]{:S(2)}, u32[]{:S(2)}) %collective-permute-start) | collective-permute-done | bytes 1048608 | tf_op jit(solution)/shard_map/ppermute | solution.py:14
  35.9 0.0 copy-done
  35.9 0.0 copy-start.2
  35.9 1.0 copy-done.2
  36.9 3.2 %collective-permute-done.1 = bf16[2048,256]{1,0:T(8,128)(2,1)} collective-permute-done((bf16[2048,256]{1,0:T(8,128)(2,1)S(1)}, bf16[2048,256]{1,0:T(8,128)(2,1)}, u32[]{:S(2)}, u32[]{:S(2)}) %collective-permute-start.1) | collective-permute-done | bytes 1048608 | tf_op jit(solution)/shard_map/ppermute | solution.py:15
  40.1 2.1 pad_maximum_fusion.1
  42.2 6.5 %gather_fusion = bf16[128,128,256]{2,1,0:T(8,128)(2,1)} fusion(bf16[48,128,256]{2,1,0:T(8,128)(2,1)S(1)} %bitcast.29, s32[1024]{0:T(1024)S(1)} %pad_clamp_fusion), kind=kCustom, calls=%fused_computation | custom fusion | bytes 16777728 | tf_op jit(solution)/shard_map/gather | solution.py:38
  48.8 7.1 %fusion.2 = f32[16,128,256]{1,2,0:T(8,128)S(1)} fusion(bf16[16,8,128,256]{3,2,1,0:T(8,128)(2,1)} %bitcast.27, bf16[16,8,128,128]{3,2,1,0:T(8,128)(2,1)} %param.8, f32[16,128]{1,0:T(8,128)S(1)} %get-tuple-element.5), kind=kOutput, calls=%fused_computation.8 | convolution fusion | flops 1074266112 | bytes 14688256 | tf_op jit(solution)/shard_map/ikpq,ikqn->ipn/dot_general | solution.py:41
  55.8 7.1 %fusion.1 = f32[16,128,256]{1,2,0:T(8,128)S(1)} fusion(bf16[16,8,128,256]{3,2,1,0:T(8,128)(2,1)} %bitcast.28, bf16[16,8,128,128]{3,2,1,0:T(8,128)(2,1)} %param.9, f32[16,128]{1,0:T(8,128)S(1)} %get-tuple-element.5), kind=kOutput, calls=%fused_computation.6 | convolution fusion | flops 1074266112 | bytes 14688256 | tf_op jit(solution)/shard_map/ikpq,ikqn->ipn/dot_general | solution.py:45
  62.9 2.2 pad_maximum_fusion
  65.1 5.4 %copy.8 = f32[16,128,512]{2,1,0:T(8,128)} copy(f32[16,128,512]{1,2,0:T(8,128)} %pad_maximum_fusion) | data formatting | bytes 8388608 | tf_op jit(solution)/shard_map/concatenate | solution.py:48
  70.5 0.0 copy-start.1
  70.5 0.0 reduce-scatter.2.cloned.1.call-update
  70.5 0.0 all-gather.5.cloned.1.call-start
  70.6 1.1 copy-done.1
  71.7 0.8 constant_dynamic-slice_fusion
  72.5 0.0 all-gather.5.cloned.1.call-update
  72.6 0.0 all-reduce.2.cloned.1.call-start
  72.6 19.7 %reduce-scatter.2.cloned.1.call-done = f32[1024,512]{1,0:T(8,128)} async-done(((f32[2048,512]{1,0:T(8,128)}), f32[1024,512]{1,0:T(8,128)}) %reduce-scatter.2.cloned.1.call-update) | async-done | bytes 2097168 | tf_op jit(solution)/shard_map/reduce_scatter | solution.py:49
  92.3 1.7 convert.5
  94.1 64.5 %all-gather.5.cloned.1.call-done = bf16[1024,4096]{1,0:T(8,128)(2,1)} async-done(((bf16[1024,256]{1,0:T(8,128)(2,1)}), bf16[1024,4096]{1,0:T(8,128)(2,1)}) %all-gather.5.cloned.1.call-update) | async-done | bytes 8388624 | tf_op jit(solution)/shard_map/all_gather | solution.py:57
  158.6 7.8 %fusion.5 = f32[4096,256]{1,0:T(8,128)} fusion(bf16[1024,4096]{1,0:T(8,128)(2,1)} %all-gather.5.cloned.1.call-done, bf16[1024,512]{1,0:T(8,128)(2,1)S(1)} %convert.5), kind=kOutput, calls=%fused_computation.12 | convolution fusion | flops 2147483648 | bytes 13107200 | tf_op jit(solution)/shard_map/dot_general | solution.py:56
  166.4 0.0 all-reduce.2.cloned.1.call-update
  166.4 0.0 all-gather.3.cloned.1.call-start
  166.5 0.8 slice.13
  167.3 0.0 all-gather.3.cloned.1.call-update
  167.3 121.5 %all-reduce.2.cloned.1.call-done = f32[4096,256]{1,0:T(8,128)} async-done(((f32[4096,256]{1,0:T(8,128)}), f32[4096,256]{1,0:T(8,128)}) %all-reduce.2.cloned.1.call-update) | async-done | bytes 4194320 | tf_op jit(solution)/shard_map/psum | solution.py:62
  288.9 0.0 all-gather.3.cloned.1.call-done
  288.9 7.9 %fusion.4 = f32[1024,256]{1,0:T(8,128)} fusion(bf16[1024,4096]{1,0:T(8,128)(2,1)} %all-gather.3.cloned.1.call-done, f32[4096,256]{1,0:T(8,128)} %all-reduce.2.cloned.1.call-done, bf16[1024,512]{1,0:T(8,128)(2,1)S(1)} %convert.5), kind=kOutput, calls=%fused_computation.10 | convolution fusion | flops 2150105088 | bytes 14155776 | tf_op jit(solution)/shard_map/dot_general | solution.py:64
  (1 shorter events, 0.0 us)
Async XLA Ops:
  7.4 85.0 %reduce-scatter.2.cloned.1.call-start = ((), (), s32[]{:S(2)}) async-start(), calls=%async_computation.1 | async-start | bytes 6291456 | tf_op jit(solution)/shard_map/reduce_scatter | solution.py:49
  9.7 26.2 %copy-start = (bf16[2048,256]{1,0:T(8,128)(2,1)}, bf16[2048,256]{1,0:T(8,128)(2,1)S(1)}, u32[]{:S(2)}) copy-start(bf16[2048,256]{1,0:T(8,128)(2,1)S(1)} %broadcast_multiply_fusion) | copy-start | bytes 3145732
  9.7 26.2 %collective-permute-start = (bf16[2048,256]{1,0:T(8,128)(2,1)S(1)}, bf16[2048,256]{1,0:T(8,128)(2,1)S(1)}, u32[]{:S(2)}, u32[]{:S(2)}) collective-permute-start(bf16[2048,256]{1,0:T(8,128)(2,1)S(1)} %broadcast_multiply_fusion), channel_id=1, source_target_pairs={{0,32},{32,64},{64,96},{96,128},{128,160},{160,192},{192,224},{1,3... | collective-permute-start | bytes 3145736 | tf_op jit(solution)/shard_map/ppermute | solution.py:14
  14.1 26.0 %collective-permute-start.1 = (bf16[2048,256]{1,0:T(8,128)(2,1)S(1)}, bf16[2048,256]{1,0:T(8,128)(2,1)}, u32[]{:S(2)}, u32[]{:S(2)}) collective-permute-start(bf16[2048,256]{1,0:T(8,128)(2,1)S(1)} %broadcast_multiply_fusion), channel_id=1, source_target_pairs={{32,0},{64,32},{96,64},{128,96},{160,128},{192,160},{224,192},{33,... | collective-permute-start | bytes 3145736 | tf_op jit(solution)/shard_map/ppermute | solution.py:15
  35.9 1.0 copy-start.2
  70.5 1.2 copy-start.1
  70.5 88.1 %all-gather.5.cloned.1.call-start = ((), (), s32[]{:S(2)}) async-start(), calls=%async_computation.3 | async-start | bytes 8912896 | tf_op jit(solution)/shard_map/all_gather | solution.py:57
  72.6 216.3 %all-reduce.2.cloned.1.call-start = ((), (), s32[]{:S(2)}) async-start(), calls=%async_computation.4 | async-start | bytes 8388608 | tf_op jit(solution)/shard_map/psum | solution.py:62
  166.4 122.4 %all-gather.3.cloned.1.call-start = ((), (), s32[]{:S(2)}) async-start(), calls=%async_computation.2 | async-start | bytes 8912896 | tf_op jit(solution)/shard_map/all_gather | solution.py:65
Sparse Core Ops, SparseCore 0:
  70.6 21.6 reduce-scatter.1
  166.5 122.2 all-reduce.1
Sparse Core Ops, SparseCore 1:
  73.4 85.2 all-gather.4
  169.6 82.0 all-gather.2
where the time goes:
time: 305 us; the launch traced here: 304 us
  waiting for transfers between devices  229 us (75%)
  matrix products  29.8 us (10%)
  local copies, waits for them, and re-layouts  15.8 us (5%)
  between operations  14.9 us (5%)
  other arithmetic  9.15 us (3%)
  starting transfers between devices  5.86 us (2%)
    psum x1, waiting for transfers between devices, body(): whole_gram = lax.psum(partial_gram, ('row', 'layer'))  122 us
    all_gather x1, waiting for transfers between devices, body(): lax.all_gather(masked_half, 'col', axis=1, tiled=True)  64.5 us
    reduce_scatter x1, waiting for transfers between devices, body(): lax.psum_scatter(both.reshape(nsel * block_rows, 2 * cols_dev), 'layer',...  19.7 us
    ppermute x1, waiting for transfers between devices, padded_2(): before = lax.ppermute(last, axis, up)  19.6 us
    dot_general x1, matrix products, body(): jnp.dot(lax.all_gather(sc_half, 'col', axis=1, tiled=True), gram, preferr...  7.88 us
    dot_general x1, matrix products, body(): lax.dot_general(lax.all_gather(masked_half, 'col', axis=1, tiled=True), h...  7.79 us
    dot_general x1, matrix products, body(): jnp.einsum('ikpq,ikqn->ipn', ovl_blocks, picked, preferred_element_type=j...  7.05 us
    dot_general x1, matrix products, body(): jnp.einsum('ikpq,ikqn->ipn', ham_blocks, picked, preferred_element_type=j...  7.05 us
  transfers between devices with their start and end apart: 6, of which 5 were waited for; matrix products, arithmetic and copies ran while one was open for 1% of the time, Pallas kernels for 0%

commit v1 on v0

v1 whole, which is shorter than its diff:
```python
import jax
import jax.numpy as jnp
from jax import lax
from jax.experimental import pallas as pl
from jax.experimental.pallas import tpu as pltpu
from jax.sharding import PartitionSpec as P

MESH = pl.DeviceIdType.MESH
BF = jnp.bfloat16
F32 = jnp.float32
GROUPS = ((0, 1), (2, 3))


def kernel(
    sizes, neigh, coeffs, ham, ovl, out,
    raw, cbuf, hbuf, sbuf, ctg, hcg, scg, gown, gsend, grecv, gram,
    rs_s, rs_r, rs_s4, rs_r4, opp_s, opp_r, nb_s, nb_r, racc,
    loc, zs, zr, hs, hr, ys, yr, xs, xr, ss, sr, ps, pr,
    rss, rsr, ags, agr, agps, agpr, fs, fr,
):
    z = lax.axis_index("row")
    col = lax.axis_index("col")
    l = lax.axis_index("layer")
    x, y = col // 4, col % 4
    here = (z, col, l)
    up = (lax.rem(z + 1, 8), col, l)
    down = (lax.rem(z + 7, 8), col, l)
    xr_dev = (z, lax.rem(x + 1, 4) * 4 + y, l)
    xl_dev = (z, lax.rem(x + 3, 4) * 4 + y, l)
    yr_dev = (z, x * 4 + lax.rem(y + 1, 4), l)
    yl_dev = (z, x * 4 + lax.rem(y + 3, 4), l)
    twin = (z, col, 1 - l)
    del here

    def remote(src, dst, s, r, device):
        return pltpu.make_async_remote_copy(
            src_ref=src, dst_ref=dst, send_sem=s, recv_sem=r, device_id=device, device_id_type=MESH
        )

    sent = []

    def send(src, dst, s, r, device):
        copy = remote(src, dst, s, r, device)
        copy.start()
        sent.append(copy)
        return copy

    load = pltpu.make_async_copy(coeffs, raw, loc.at[0])
    load.start()
    barrier = pltpu.get_barrier_semaphore()
    for device in (up, down, xr_dev, xl_dev, yr_dev, yl_dev, twin):
        pl.semaphore_signal(barrier, inc=1, device_id=device, device_id_type=MESH)
    own_h = pltpu.make_async_copy(
        ham.at[pl.ds(l * 8, 8)], hbuf.at[:, pl.ds(l * 8, 8)], loc.at[1]
    )
    own_s = pltpu.make_async_copy(
        ovl.at[pl.ds(l * 8, 8)], sbuf.at[:, pl.ds(l * 8, 8)], loc.at[2]
    )
    load.wait()

    def mask_block(b):
        block = raw[pl.ds(b * 128, 128), :].astype(F32)
        rows = lax.broadcasted_iota(jnp.int32, (128, 256), 0)
        cbuf[16 + b] = jnp.where(rows < sizes[b], block, 0.0).astype(BF)

    @pl.loop(0, 8)
    def _(i):
        mask_block(l * 8 + i)

    pl.semaphore_wait(barrier, 7)

    mine = cbuf.at[pl.ds(16 + l * 8, 8)]
    to_up = send(mine, cbuf.at[pl.ds(l * 8, 8)], zs.at[0], zr.at[0], up)
    to_down = send(mine, cbuf.at[pl.ds(32 + l * 8, 8)], zs.at[1], zr.at[1], down)
    give_h = send(
        ham.at[pl.ds((1 - l) * 8, 8)], hbuf.at[:, pl.ds(l * 8, 8)], hs.at[0], hr.at[0], twin
    )
    own_h.start()

    @pl.loop(0, 8)
    def _(i):
        ctg[y, :, pl.ds(pl.multiple_of(i * 128, 128), 128)] = cbuf[16 + l * 8 + i].T

    def ring4(buf, me, half, s, r, right, left):
        a, b = pl.ds(0, half), pl.ds(half, half)
        fa = lax.rem(me + 3, 4)
        fb = lax.rem(me + 1, 4)
        ra = send(buf.at[me, a], buf.at[me, a], s.at[0], r.at[0], right)
        lb = send(buf.at[me, b], buf.at[me, b], s.at[1], r.at[1], left)
        yield
        rb = send(buf.at[me, b], buf.at[me, b], s.at[2], r.at[2], right)
        la = send(buf.at[me, a], buf.at[me, a], s.at[3], r.at[3], left)
        yield
        ra.wait_recv()
        fra = send(buf.at[fa, a], buf.at[fa, a], s.at[4], r.at[4], right)
        lb.wait_recv()
        flb = send(buf.at[fb, b], buf.at[fb, b], s.at[5], r.at[5], left)
        yield
        rb.wait_recv()
        la.wait_recv()
        yield
        fra.wait_recv()
        flb.wait_recv()
        yield

    yring = ring4(ctg, y, 128, ys, yr, yr_dev, yl_dev)
    next(yring)
    next(yring)
    give_s = send(
        ovl.at[pl.ds((1 - l) * 8, 8)], sbuf.at[:, pl.ds(l * 8, 8)], hs.at[1], hr.at[1], twin
    )
    own_s.start()

    @pl.loop(0, 8)
    def _(i):
        mask_block((1 - l) * 8 + i)

    next(yring)
    to_up.wait_recv()
    to_down.wait_recv()
    hand = jnp.where(l == 0, 32, 8)
    take = send(cbuf.at[pl.ds(hand, 8)], cbuf.at[pl.ds(hand, 8)], zs.at[2], zr.at[2], twin)
    own_h.wait()
    give_h.wait_recv()
    take.wait_recv()

    first = z * 16 - 16

    def picked(b, k):
        return cbuf[jnp.clip(neigh[b, k] - first, 0, 47)]

    def spmm(blocks, store, begin, end):
        @pl.loop(begin, end)
        def _(i):
            b = l * 8 + i
            total = jnp.zeros((128, 256), F32)
            for k in range(0, 16, 2):
                lhs = jnp.concatenate([blocks[i, k], blocks[i, k + 1]], axis=1)
                rhs = jnp.concatenate([picked(b, k), picked(b, k + 1)], axis=0)
                total += jnp.dot(lhs, rhs, preferred_element_type=F32)
            rows = lax.broadcasted_iota(jnp.int32, (128, 256), 0)
            store[pl.ds(pl.multiple_of(i * 128, 128), 128), :] = jnp.where(
                rows < sizes[b], total, 0.0
            ).astype(BF)

    spmm(hbuf, hcg.at[x], 0, 8)
    xring = ring4(hcg, x, 512, xs, xr, xr_dev, xl_dev)
    next(xring)
    next(xring)
    next(yring)
    next(yring)
    own_s.wait()
    give_s.wait_recv()
    spmm(sbuf, scg.at[y], 0, 8)
    sring = ring4(scg, y, 512, ss, sr, yr_dev, yl_dev)
    next(sring)
    next(sring)

    slots = (x, lax.rem(x + 2, 4), lax.rem(x + 1, 4), lax.rem(x + 3, 4))
    swaps = {}

    def gram_part(p):
        rhs = hcg.at[slots[p]]

        @pl.loop(0, 2)
        def _(i):
            gsend[p, pl.ds(pl.multiple_of(i * 256, 256), 256), :] = jnp.dot(
                ctg[(1 - l) * 2 + i], rhs[...], preferred_element_type=F32
            )

        swaps[p] = send(gsend.at[p], grecv.at[p], ps.at[p], pr.at[p], twin)

        @pl.loop(0, 2)
        def _(i):
            gown[p, pl.ds(pl.multiple_of(i * 256, 256), 256), :] = jnp.dot(
                ctg[l * 2 + i], rhs[...], preferred_element_type=F32
            )

    def gram_add(p):
        swaps[p].wait_recv()
        gown[p] = gown[p] + grecv[p]

    def part(g, d):
        c = lax.rem(z + 8 + d, 8)
        return gown[g[0] : g[-1] + 1, pl.ds(pl.multiple_of(c * 64, 64), 64), :]

    def z_reduce(gi):
        g = GROUPS[gi]
        where = pl.ds(g[0], len(g))
        for p in g:
            gram_add(p)
        rs_s4[0, where] = part(g, 4)[:, :, :128].astype(BF)
        rs_s4[1, where] = part(g, 4)[:, :, 128:].astype(BF)
        right = send(rs_s4.at[0, where], rs_r4.at[0, where], rss.at[gi, 0], rsr.at[gi, 0], up)
        left = send(rs_s4.at[1, where], rs_r4.at[1, where], rss.at[gi, 1], rsr.at[gi, 1], down)
        for k in range(3):
            yield
            d = 3 - k
            right.wait_recv()
            term = part(g, d)
            if k == 0:
                rs_s[k, 0, where, :, :128] = (
                    term[:, :, :128] + rs_r4[0, where].astype(F32)
                ).astype(BF)
                rs_s[k, 0, where, :, 128:] = term[:, :, 128:].astype(BF)
            else:
                rs_s[k, 0, where] = (term + rs_r[k - 1, 0, where].astype(F32)).astype(BF)
            right = send(
                rs_s.at[k, 0, where], rs_r.at[k, 0, where],
                rss.at[gi, 2 * k + 2], rsr.at[gi, 2 * k + 2], up,
            )
            left.wait_recv()
            term = part(g, -d)
            if k == 0:
                rs_s[k, 1, where, :, 128:] = (
                    term[:, :, 128:] + rs_r4[1, where].astype(F32)
                ).astype(BF)
                rs_s[k, 1, where, :, :128] = term[:, :, :128].astype(BF)
            else:
                rs_s[k, 1, where] = (term + rs_r[k - 1, 1, where].astype(F32)).astype(BF)
            left = send(
                rs_s.at[k, 1, where], rs_r.at[k, 1, where],
                rss.at[gi, 2 * k + 3], rsr.at[gi, 2 * k + 3], down,
            )
        yield
        right.wait_recv()
        left.wait_recv()
        whole = part(g, 0) + rs_r[2, 0, where].astype(F32) + rs_r[2, 1, where].astype(F32)

        def rows(d):
            c = lax.rem(z + 8 + d, 8)
            return pl.ds(pl.multiple_of(l * 512 + c * 64, 64), 64)

        gram[where, rows(0), :] = (whole * (1.0 / 16384.0)).astype(BF)
        twins = []

        def to_twin(d, n):
            ref = gram.at[where, rows(d), :]
            twins.append(send(ref, ref, agps.at[gi, n], agpr.at[gi, n], twin))

        def hop(d, n, device, cols=slice(None)):
            ref = gram.at[where, rows(d), cols]
            return send(ref, ref, ags.at[gi, n], agr.at[gi, n], device)

        right = hop(0, 0, up)
        left = hop(0, 1, down)
        to_twin(0, 0)
        for k in range(1, 4):
            yield
            right.wait_recv()
            right = hop(-k, 2 * k, up, slice(None) if k < 3 else pl.ds(0, 128))
            to_twin(-k, 2 * k - 1)
            left.wait_recv()
            left = hop(k, 2 * k + 1, down, slice(None) if k < 3 else pl.ds(128, 128))
            to_twin(k, 2 * k)
        yield
        right.wait_recv()
        left.wait_recv()
        to_twin(4, 7)
        yield
        for copy in twins:
            copy.wait_recv()
        yield

    def drain(gen):
        for _ in gen:
            pass

    gram_part(0)
    next(xring)
    next(sring)
    next(xring)
    next(xring)
    gram_part(1)
    zr0 = z_reduce(0)
    next(zr0)
    gram_part(2)
    gram_part(3)
    next(zr0)
    zr1 = z_reduce(1)
    next(zr1)
    next(zr0)
    next(zr1)
    next(sring)
    next(sring)
    for _ in range(8):
        next(zr0, None)
        next(zr1, None)
    drain(zr0)

    def project(p, i):
        total = jnp.zeros((512, 256), F32)
        for k in range(4):
            total += jnp.dot(
                scg[k, pl.ds(i * 512, 512), :], gram[p, k * 256 : (k + 1) * 256, :],
                preferred_element_type=F32,
            )
        return total

    opp_s[0] = project(1, 0).astype(BF)
    far_r = send(opp_s.at[0], opp_r.at[0], fs.at[0], fr.at[0], xr_dev)
    opp_s[1] = project(1, 1).astype(BF)
    far_l = send(opp_s.at[1], opp_r.at[1], fs.at[1], fr.at[1], xl_dev)
    drain(zr1)
    nb_s[0, 1] = project(2, 1).astype(BF)
    near = [send(nb_s.at[0, 1], nb_r.at[0, 1], fs.at[2], fr.at[2], xr_dev)]
    nb_s[1, 0] = project(3, 0).astype(BF)
    near.append(send(nb_s.at[1, 0], nb_r.at[1, 0], fs.at[3], fr.at[3], xl_dev))
    racc[0] = project(2, 0)
    racc[1] = project(3, 1)
    far_r.wait_recv()
    nb_s[0, 0] = (racc[0] + opp_r[0].astype(F32)).astype(BF)
    near.append(send(nb_s.at[0, 0], nb_r.at[0, 0], fs.at[4], fr.at[4], xr_dev))
    far_l.wait_recv()
    nb_s[1, 1] = (racc[1] + opp_r[1].astype(F32)).astype(BF)
    near.append(send(nb_s.at[1, 1], nb_r.at[1, 1], fs.at[5], fr.at[5], xl_dev))
    for i in range(2):
        racc[i] = hcg[x, pl.ds(i * 512, 512), :].astype(F32) - project(0, i)
    for copy in near:
        copy.wait_recv()
    for i in range(2):
        out[pl.ds(i * 512, 512), :] = racc[i] - nb_r[0, i].astype(F32) - nb_r[1, i].astype(F32)
    for copy in sent:
        copy.wait_send()


def body(coeffs, block_sizes, neighbours, ham_blocks, ovl_blocks):
    vmem = pltpu.VMEM
    dma = pltpu.SemaphoreType.DMA
    n = len(GROUPS)
    smem = pl.BlockSpec(memory_space=pltpu.SMEM)
    hbm = pl.BlockSpec(memory_space=pl.ANY)
    return pl.pallas_call(
        kernel,
        out_shape=jax.ShapeDtypeStruct((1024, 256), F32),
        in_specs=[smem, smem, hbm, hbm, hbm],
        out_specs=pl.BlockSpec(memory_space=pltpu.VMEM),
        scratch_shapes=[
            vmem((2048, 256), BF),
            vmem((48, 128, 256), BF),
            vmem((8, 16, 128, 128), BF),
            vmem((8, 16, 128, 128), BF),
            vmem((4, 256, 1024), BF),
            vmem((4, 1024, 256), BF),
            vmem((4, 1024, 256), BF),
            vmem((4, 512, 256), F32),
            vmem((4, 512, 256), F32),
            vmem((4, 512, 256), F32),
            vmem((4, 1024, 256), BF),
            vmem((3, 2, 4, 64, 256), BF),
            vmem((3, 2, 4, 64, 256), BF),
            vmem((2, 4, 64, 128), BF),
            vmem((2, 4, 64, 128), BF),
            vmem((2, 512, 256), BF),
            vmem((2, 512, 256), BF),
            vmem((2, 2, 512, 256), BF),
            vmem((2, 2, 512, 256), BF),
            vmem((2, 512, 256), F32),
            dma((3,)),
            dma((3,)), dma((3,)),
            dma((2,)), dma((2,)),
            dma((6,)), dma((6,)),
            dma((6,)), dma((6,)),
            dma((6,)), dma((6,)),
            dma((4,)), dma((4,)),
            dma((n, 8)), dma((n, 8)),
            dma((n, 8)), dma((n, 8)),
            dma((n, 8)), dma((n, 8)),
            dma((6,)), dma((6,)),
        ],
        compiler_params=pltpu.CompilerParams(
            collective_id=0, has_side_effects=True, vmem_limit_bytes=56 * 2**20
        ),
        cost_estimate=pl.CostEstimate(
            flops=6 * 2**30, bytes_accessed=12 * 2**20, transcendentals=0
        ),
        name="block_sparse_residual",
    )(block_sizes, neighbours, coeffs, ham_blocks, ovl_blocks)


def solution(mesh):
    return jax.shard_map(
        body,
        mesh=mesh,
        in_specs=(
            P("row", "col"),
            P("row"),
            P("row", None),
            P("row", "layer", None, None),
            P("row", "layer", None, None),
        ),
        out_specs=P(("row", "layer"), "col"),
        check_vma=False,
    )
```

time: 305 us -> 108 us (0.35)
  waiting for transfers between devices: 229 us -> 0 us
  Pallas kernels: 0 us -> 105 us
  matrix products: 29.8 us -> 0 us
  between operations: 14.9 us -> 0.01 us
  local copies, waits for them, and re-layouts: 15.8 us -> 2.26 us
  other arithmetic: 9.15 us -> 0 us
  starting transfers between devices: 5.86 us -> 0 us
    psum x1 -> x0, waiting for transfers between devices: 122 us -> none  [body(): whole_gram = lax.psum(partial_gram, ('row', 'layer'))]
    pallas_call x0 -> x1, Pallas kernels: none -> 105 us  [body(): pl.pallas_call(kernel, out_shape=jax.ShapeDtypeStruct((1024, 256), F32),...]
    all_gather x2 -> x0, waiting for transfers between devices: 64.5 us -> none  [the longest x1 64.5 us: body(): lax.all_gather(masked_half, 'col', axis=1, tiled=True)]
    dot_general x4 -> x0, matrix products: 29.8 us -> none  [the longest x1 7.88 us: body(): jnp.dot(lax.all_gather(sc_half, 'col', axis=1, tiled=True), gram, preferr...]
    ppermute x2 -> x0, waiting for transfers between devices: 22.8 us -> none  [the longest x1 19.6 us: padded_2(): before = lax.ppermute(last, axis, up)]
    reduce_scatter x1 -> x0, waiting for transfers between devices: 19.7 us -> none  [body(): lax.psum_scatter(both.reshape(nsel * block_rows, 2 * cols_dev), 'layer',...]
    gather x1 -> x0, local copies, waits for them, and re-layouts: 6.55 us -> none  [body(): picked = padded[layer_neigh - first_block]]
    ppermute x2 -> x0, starting transfers between devices: 5.73 us -> none  [the longest x1 4.44 us: padded_2(): before = lax.ppermute(last, axis, up)]
  transfers between devices with their start and end apart: 6 -> 0, of which waited for: 5 -> 0; matrix products, arithmetic and copies ran while one was open for 1% -> 0% of each run, Pallas kernels for 0% -> 0%
where the time goes in v1:
time: 108 us
  Pallas kernels  105 us (97%)
  local copies, waits for them, and re-layouts  2.26 us (2%)
    pallas_call x1, Pallas kernels, body(): pl.pallas_call(kernel, out_shape=jax.ShapeDtypeStruct((1024, 256), F32),...  105 us
    unnamed x1, local copies, waits for them, and re-layouts  2.26 us

profile of v1, /device:TPU:1, one launch (start us, length us, event | category | flops | bytes accessed | tf_op | source)
XLA Modules:
  0.0 107.6 jit_solution(1426137110280388706)
XLA Ops:
  0.0 105.3 %block_sparse_residual.1 = f32[1024,256]{1,0:T(8,128)} custom-call(s32[16]{0:T(128)} %sizes.1, s32[16,16]{1,0:T(8,128)} %neigh.1, bf16[2048,256]{1,0:T(8,128)(2,1)} %coeffs.1, bf16[16,8,128,128]{3,2,1,0:T(8,128)(2,1)} %ham.1, bf16[16,8,128,128]{3,2,1,0:T(8,128)(2,1)} %ovl.1), custom_call_target="tpu_custom_call" | custom-call | flops 6442450944 | bytes 12582912 | tf_op jit(solution)/shard_map/block_sparse_residual/pallas_call | solution.py:333
  105.3 2.3 %copy.7 = f32[1024,256]{1,0:T(8,128)} copy(f32[1024,256]{1,0:T(8,128)} %block_sparse_residual.1) | data formatting | bytes 2097152

commit v2 on v1

--- a/solution.py
+++ b/solution.py
@@ -8,13 +8,13 @@
 MESH = pl.DeviceIdType.MESH
 BF = jnp.bfloat16
 F32 = jnp.float32
-GROUPS = ((0, 1), (2, 3))
+GROUPS = ((0,), (1,), (2,), (3,))
 
 
 def kernel(
     sizes, neigh, coeffs, ham, ovl, out,
     raw, cbuf, hbuf, sbuf, ctg, hcg, scg, gown, gsend, grecv, gram,
-    rs_s, rs_r, rs_s4, rs_r4, opp_s, opp_r, nb_s, nb_r, racc,
+    rs_s, rs_r, rs_s4, rs_r4, opp_s, opp_r, nb_s, nb_r, racc, own,
     loc, zs, zr, hs, hr, ys, yr, xs, xr, ss, sr, ps, pr,
     rss, rsr, ags, agr, agps, agpr, fs, fr,
 ):
@@ -39,6 +39,10 @@
 
     sent = []
 
+    def gone(copy):
+        copy.wait_send()
+        sent[:] = [other for other in sent if other is not copy]
+
     def send(src, dst, s, r, device):
         copy = remote(src, dst, s, r, device)
         copy.start()
@@ -101,6 +105,31 @@
         yield
         fra.wait_recv()
         flb.wait_recv()
+        yield
+
+    def ring4x(buf, me, half, s, r, right, left):
+        a, b = pl.ds(0, half), pl.ds(half, half)
+        fa = lax.rem(me + 3, 4)
+        fb = lax.rem(me + 1, 4)
+        ra = send(buf.at[me, a], buf.at[me, a], s.at[0], r.at[0], right)
+        yield
+        lb = send(buf.at[me, b], buf.at[me, b], s.at[1], r.at[1], left)
+        yield
+        ra.wait_recv()
+        fra = send(buf.at[fa, a], buf.at[fa, a], s.at[2], r.at[2], right)
+        lb.wait_recv()
+        flb = send(buf.at[fb, b], buf.at[fb, b], s.at[3], r.at[3], left)
+        yield
+        gone(fra)
+        rb = send(buf.at[me, b], buf.at[me, b], s.at[4], r.at[4], right)
+        gone(flb)
+        la = send(buf.at[me, a], buf.at[me, a], s.at[5], r.at[5], left)
+        yield
+        fra.wait_recv()
+        flb.wait_recv()
+        yield
+        rb.wait_recv()
+        la.wait_recv()
         yield
 
     yring = ring4(ctg, y, 128, ys, yr, yr_dev, yl_dev)
@@ -142,19 +171,6 @@
             store[pl.ds(pl.multiple_of(i * 128, 128), 128), :] = jnp.where(
                 rows < sizes[b], total, 0.0
             ).astype(BF)
-
-    spmm(hbuf, hcg.at[x], 0, 8)
-    xring = ring4(hcg, x, 512, xs, xr, xr_dev, xl_dev)
-    next(xring)
-    next(xring)
-    next(yring)
-    next(yring)
-    own_s.wait()
-    give_s.wait_recv()
-    spmm(sbuf, scg.at[y], 0, 8)
-    sring = ring4(scg, y, 512, ss, sr, yr_dev, yl_dev)
-    next(sring)
-    next(sring)
 
     slots = (x, lax.rem(x + 2, 4), lax.rem(x + 1, 4), lax.rem(x + 3, 4))
     swaps = {}
@@ -262,31 +278,48 @@
             copy.wait_recv()
         yield
 
-    def drain(gen):
-        for _ in gen:
-            pass
-
+    spmm(hbuf, hcg.at[x], 0, 4)
+    xring = ring4x(hcg, x, 512, xs, xr, xr_dev, xl_dev)
+    next(xring)
+    spmm(hbuf, hcg.at[x], 4, 8)
+    next(xring)
+    next(yring)
+    next(yring)
+    own_s.wait()
+    give_s.wait_recv()
     gram_part(0)
-    next(xring)
+    spmm(sbuf, scg.at[y], 0, 8)
+    sring = ring4(scg, y, 512, ss, sr, yr_dev, yl_dev)
     next(sring)
-    next(xring)
+    next(sring)
+    reducers = [z_reduce(gi) for gi in range(4)]
+
+    def step(*which):
+        for gi in which:
+            next(reducers[gi])
+
+    step(0)
+    next(xring)
+    step(0, 0)
+    next(xring)
+    step(0)
     next(xring)
     gram_part(1)
-    zr0 = z_reduce(0)
-    next(zr0)
+    step(0, 1, 0, 1)
+    next(sring)
+    next(xring)
     gram_part(2)
     gram_part(3)
-    next(zr0)
-    zr1 = z_reduce(1)
-    next(zr1)
-    next(zr0)
-    next(zr1)
+    step(1, 2, 3, 0)
+    for _ in range(2):
+        step(1, 2, 3, 0)
+    step(0)
+    for _ in range(2):
+        step(1, 2, 3)
     next(sring)
     next(sring)
-    for _ in range(8):
-        next(zr0, None)
-        next(zr1, None)
-    drain(zr0)
+    for _ in range(3):
+        step(1, 2, 3)
 
     def project(p, i):
         total = jnp.zeros((512, 256), F32)
@@ -301,7 +334,10 @@
     far_r = send(opp_s.at[0], opp_r.at[0], fs.at[0], fr.at[0], xr_dev)
     opp_s[1] = project(1, 1).astype(BF)
     far_l = send(opp_s.at[1], opp_r.at[1], fs.at[1], fr.at[1], xl_dev)
-    drain(zr1)
+    step(2, 3)
+    for i in range(2):
+        own[i] = hcg[x, pl.ds(i * 512, 512), :].astype(F32) - project(0, i)
+    step(2, 3)
     nb_s[0, 1] = project(2, 1).astype(BF)
     near = [send(nb_s.at[0, 1], nb_r.at[0, 1], fs.at[2], fr.at[2], xr_dev)]
     nb_s[1, 0] = project(3, 0).astype(BF)
@@ -314,12 +350,10 @@
     far_l.wait_recv()
     nb_s[1, 1] = (racc[1] + opp_r[1].astype(F32)).astype(BF)
     near.append(send(nb_s.at[1, 1], nb_r.at[1, 1], fs.at[5], fr.at[5], xl_dev))
-    for i in range(2):
-        racc[i] = hcg[x, pl.ds(i * 512, 512), :].astype(F32) - project(0, i)
     for copy in near:
         copy.wait_recv()
     for i in range(2):
-        out[pl.ds(i * 512, 512), :] = racc[i] - nb_r[0, i].astype(F32) - nb_r[1, i].astype(F32)
+        out[pl.ds(i * 512, 512), :] = own[i] - nb_r[0, i].astype(F32) - nb_r[1, i].astype(F32)
     for copy in sent:
         copy.wait_send()
 
@@ -356,6 +390,7 @@
             vmem((2, 2, 512, 256), BF),
             vmem((2, 2, 512, 256), BF),
             vmem((2, 512, 256), F32),
+            vmem((2, 512, 256), F32),
             dma((3,)),
             dma((3,)), dma((3,)),
             dma((2,)), dma((2,)),

time: 108 us -> 103 us (0.954)
  Pallas kernels: 105 us -> 101 us
    pallas_call x1, Pallas kernels: 105 us -> 101 us  [body(): pl.pallas_call(kernel, out_shape=jax.ShapeDtypeStruct((1024, 256), F32),...]
where the time goes in v2:
time: 103 us
  Pallas kernels  101 us (98%)
  local copies, waits for them, and re-layouts  2.26 us (2%)
    pallas_call x1, Pallas kernels, body(): pl.pallas_call(kernel, out_shape=jax.ShapeDtypeStruct((1024, 256), F32),...  101 us
    unnamed x1, local copies, waits for them, and re-layouts  2.26 us

profile of v2, /device:TPU:1, one launch (start us, length us, event | category | flops | bytes accessed | tf_op | source)
XLA Modules:
  0.0 103.2 jit_solution(18364863934746009264)
XLA Ops:
  0.0 100.9 %block_sparse_residual.1 = f32[1024,256]{1,0:T(8,128)} custom-call(s32[16]{0:T(128)} %sizes.1, s32[16,16]{1,0:T(8,128)} %neigh.1, bf16[2048,256]{1,0:T(8,128)(2,1)} %coeffs.1, bf16[16,8,128,128]{3,2,1,0:T(8,128)(2,1)} %ham.1, bf16[16,8,128,128]{3,2,1,0:T(8,128)(2,1)} %ovl.1), custom_call_target="tpu_custom_call" | custom-call | flops 6442450944 | bytes 12582912 | tf_op jit(solution)/shard_map/block_sparse_residual/pallas_call | solution.py:367
  100.9 2.3 %copy.7 = f32[1024,256]{1,0:T(8,128)} copy(f32[1024,256]{1,0:T(8,128)} %block_sparse_residual.1) | data formatting | bytes 2097152

commit v3 on v2

--- a/solution.py
+++ b/solution.py
@@ -25,6 +25,8 @@
     here = (z, col, l)
     up = (lax.rem(z + 1, 8), col, l)
     down = (lax.rem(z + 7, 8), col, l)
+    up2 = (lax.rem(z + 2, 8), col, l)
+    down2 = (lax.rem(z + 6, 8), col, l)
     xr_dev = (z, lax.rem(x + 1, 4) * 4 + y, l)
     xl_dev = (z, lax.rem(x + 3, 4) * 4 + y, l)
     yr_dev = (z, x * 4 + lax.rem(y + 1, 4), l)
@@ -52,7 +54,7 @@
     load = pltpu.make_async_copy(coeffs, raw, loc.at[0])
     load.start()
     barrier = pltpu.get_barrier_semaphore()
-    for device in (up, down, xr_dev, xl_dev, yr_dev, yl_dev, twin):
+    for device in (up, down, up2, down2, xr_dev, xl_dev, yr_dev, yl_dev, twin):
         pl.semaphore_signal(barrier, inc=1, device_id=device, device_id_type=MESH)
     own_h = pltpu.make_async_copy(
         ham.at[pl.ds(l * 8, 8)], hbuf.at[:, pl.ds(l * 8, 8)], loc.at[1]
@@ -71,7 +73,7 @@
     def _(i):
         mask_block(l * 8 + i)
 
-    pl.semaphore_wait(barrier, 7)
+    pl.semaphore_wait(barrier, 9)
 
     mine = cbuf.at[pl.ds(16 + l * 8, 8)]
     to_up = send(mine, cbuf.at[pl.ds(l * 8, 8)], zs.at[0], zr.at[0], up)
@@ -205,43 +207,45 @@
         where = pl.ds(g[0], len(g))
         for p in g:
             gram_add(p)
-        rs_s4[0, where] = part(g, 4)[:, :, :128].astype(BF)
-        rs_s4[1, where] = part(g, 4)[:, :, 128:].astype(BF)
-        right = send(rs_s4.at[0, where], rs_r4.at[0, where], rss.at[gi, 0], rsr.at[gi, 0], up)
-        left = send(rs_s4.at[1, where], rs_r4.at[1, where], rss.at[gi, 1], rsr.at[gi, 1], down)
-        for k in range(3):
-            yield
-            d = 3 - k
-            right.wait_recv()
-            term = part(g, d)
-            if k == 0:
-                rs_s[k, 0, where, :, :128] = (
-                    term[:, :, :128] + rs_r4[0, where].astype(F32)
-                ).astype(BF)
-                rs_s[k, 0, where, :, 128:] = term[:, :, 128:].astype(BF)
-            else:
-                rs_s[k, 0, where] = (term + rs_r[k - 1, 0, where].astype(F32)).astype(BF)
-            right = send(
-                rs_s.at[k, 0, where], rs_r.at[k, 0, where],
-                rss.at[gi, 2 * k + 2], rsr.at[gi, 2 * k + 2], up,
-            )
-            left.wait_recv()
-            term = part(g, -d)
-            if k == 0:
-                rs_s[k, 1, where, :, 128:] = (
-                    term[:, :, 128:] + rs_r4[1, where].astype(F32)
-                ).astype(BF)
-                rs_s[k, 1, where, :, :128] = term[:, :, :128].astype(BF)
-            else:
-                rs_s[k, 1, where] = (term + rs_r[k - 1, 1, where].astype(F32)).astype(BF)
-            left = send(
-                rs_s.at[k, 1, where], rs_r.at[k, 1, where],
-                rss.at[gi, 2 * k + 3], rsr.at[gi, 2 * k + 3], down,
-            )
-        yield
-        right.wait_recv()
-        left.wait_recv()
-        whole = part(g, 0) + rs_r[2, 0, where].astype(F32) + rs_r[2, 1, where].astype(F32)
+        first = []
+        for side, sign, one, two in ((0, 1, up, up2), (1, -1, down, down2)):
+            rs_s[side, 0, where] = part(g, 3 * sign).astype(BF)
+            rs_s4[side, where] = part(g, 4)[:, :, side * 128 : side * 128 + 128].astype(BF)
+            n = 4 * side
+            first.append((
+                send(rs_s.at[side, 0, where], rs_r.at[side, 0, where], rss.at[gi, n], rsr.at[gi, n], one),
+                send(rs_s4.at[side, where], rs_r4.at[side, where], rss.at[gi, n + 1], rsr.at[gi, n + 1], two),
+            ))
+        near = []
+        for side, sign, one in ((0, 1, up), (1, -1, down)):
+            rs_s[side, 1, where] = part(g, sign).astype(BF)
+            n = 4 * side + 2
+            near.append(send(
+                rs_s.at[side, 1, where], rs_r.at[side, 1, where], rss.at[gi, n], rsr.at[gi, n], one
+            ))
+        yield
+        for side, sign, two in ((0, 1, up2), (1, -1, down2)):
+            three, four = first[side]
+            lo, hi = side * 128, side * 128 + 128
+            rest = slice(128, 256) if side == 0 else slice(0, 128)
+            term = part(g, 2 * sign)
+            three.wait_recv()
+            four.wait_recv()
+            term = term + rs_r[side, 0, where].astype(F32)
+            rs_s[side, 2, where, :, lo:hi] = (
+                term[:, :, lo:hi] + rs_r4[side, where].astype(F32)
+            ).astype(BF)
+            rs_s[side, 2, where, :, rest] = term[:, :, rest].astype(BF)
+            n = 4 * side + 3
+            near.append(send(
+                rs_s.at[side, 2, where], rs_r.at[side, 2, where], rss.at[gi, n], rsr.at[gi, n], two
+            ))
+        yield
+        whole = part(g, 0)
+        for copy in near:
+            copy.wait_recv()
+        for side in range(2):
+            whole = whole + rs_r[side, 1, where].astype(F32) + rs_r[side, 2, where].astype(F32)
 
         def rows(d):
             c = lax.rem(z + 8 + d, 8)
@@ -258,20 +262,24 @@
             ref = gram.at[where, rows(d), cols]
             return send(ref, ref, ags.at[gi, n], agr.at[gi, n], device)
 
-        right = hop(0, 0, up)
-        left = hop(0, 1, down)
+        far = [hop(0, 0, up2), hop(0, 1, down2)]
+        close = [hop(0, 2, up), hop(0, 3, down)]
         to_twin(0, 0)
-        for k in range(1, 4):
-            yield
-            right.wait_recv()
-            right = hop(-k, 2 * k, up, slice(None) if k < 3 else pl.ds(0, 128))
-            to_twin(-k, 2 * k - 1)
-            left.wait_recv()
-            left = hop(k, 2 * k + 1, down, slice(None) if k < 3 else pl.ds(128, 128))
-            to_twin(k, 2 * k)
-        yield
-        right.wait_recv()
-        left.wait_recv()
+        yield
+        last = []
+        for side, sign, one, two in ((0, -1, up, up2), (1, 1, down, down2)):
+            far[side].wait_recv()
+            last.append(hop(2 * sign, 4 + side, one))
+            last.append(hop(2 * sign, 6 + side, two, pl.ds(side * 128, 128)))
+        for side, sign in ((0, -1), (1, 1)):
+            to_twin(2 * sign, 1 + side)
+            close[side].wait_recv()
+            to_twin(sign, 3 + side)
+        yield
+        for n, copy in enumerate(last):
+            copy.wait_recv()
+            if n % 2 == 0:
+                to_twin(3 if n else -3, 5 + n // 2)
         to_twin(4, 7)
         yield
         for copy in twins:
@@ -305,21 +313,18 @@
     step(0)
     next(xring)
     gram_part(1)
-    step(0, 1, 0, 1)
+    step(0, 1)
     next(sring)
+    step(0, 1)
     next(xring)
     gram_part(2)
     gram_part(3)
-    step(1, 2, 3, 0)
-    for _ in range(2):
-        step(1, 2, 3, 0)
-    step(0)
-    for _ in range(2):
-        step(1, 2, 3)
+    step(1, 2, 3)
+    step(1, 2, 3)
     next(sring)
     next(sring)
-    for _ in range(3):
-        step(1, 2, 3)
+    step(1, 2, 3)
+    step(1)
 
     def project(p, i):
         total = jnp.zeros((512, 256), F32)
@@ -337,6 +342,7 @@
     step(2, 3)
     for i in range(2):
         own[i] = hcg[x, pl.ds(i * 512, 512), :].astype(F32) - project(0, i)
+    step(2, 3)
     step(2, 3)
     nb_s[0, 1] = project(2, 1).astype(BF)
     near = [send(nb_s.at[0, 1], nb_r.at[0, 1], fs.at[2], fr.at[2], xr_dev)]
@@ -381,8 +387,8 @@
             vmem((4, 512, 256), F32),
             vmem((4, 512, 256), F32),
             vmem((4, 1024, 256), BF),
-            vmem((3, 2, 4, 64, 256), BF),
-            vmem((3, 2, 4, 64, 256), BF),
+            vmem((2, 3, 4, 64, 256), BF),
+            vmem((2, 3, 4, 64, 256), BF),
             vmem((2, 4, 64, 128), BF),
             vmem((2, 4, 64, 128), BF),
             vmem((2, 512, 256), BF),

time: 103 us -> 101 us (0.981)
  Pallas kernels: 101 us -> 98.6 us
    pallas_call x1, Pallas kernels: 101 us -> 98.6 us  [body(): pl.pallas_call(kernel, out_shape=jax.ShapeDtypeStruct((1024, 256), F32),...]
where the time goes in v3:
time: 101 us
  Pallas kernels  98.6 us (98%)
  local copies, waits for them, and re-layouts  2.26 us (2%)
    pallas_call x1, Pallas kernels, body(): pl.pallas_call(kernel, out_shape=jax.ShapeDtypeStruct((1024, 256), F32),...  98.6 us
    unnamed x1, local copies, waits for them, and re-layouts  2.26 us

profile of v3, /device:TPU:1, one launch (start us, length us, event | category | flops | bytes accessed | tf_op | source)
XLA Modules:
  0.0 100.9 jit_solution(10721036504064377046)
XLA Ops:
  0.0 98.6 %block_sparse_residual.1 = f32[1024,256]{1,0:T(8,128)} custom-call(s32[16]{0:T(128)} %sizes.1, s32[16,16]{1,0:T(8,128)} %neigh.1, bf16[2048,256]{1,0:T(8,128)(2,1)} %coeffs.1, bf16[16,8,128,128]{3,2,1,0:T(8,128)(2,1)} %ham.1, bf16[16,8,128,128]{3,2,1,0:T(8,128)(2,1)} %ovl.1), custom_call_target="tpu_custom_call" | custom-call | flops 6442450944 | bytes 12582912 | tf_op jit(solution)/shard_map/block_sparse_residual/pallas_call | solution.py:373
  98.6 2.3 %copy.7 = f32[1024,256]{1,0:T(8,128)} copy(f32[1024,256]{1,0:T(8,128)} %block_sparse_residual.1) | data formatting | bytes 2097152

commit v4 on v3

--- a/solution.py
+++ b/solution.py
@@ -41,10 +41,6 @@
 
     sent = []
 
-    def gone(copy):
-        copy.wait_send()
-        sent[:] = [other for other in sent if other is not copy]
-
     def send(src, dst, s, r, device):
         copy = remote(src, dst, s, r, device)
         copy.start()
@@ -107,31 +103,6 @@
         yield
         fra.wait_recv()
         flb.wait_recv()
-        yield
-
-    def ring4x(buf, me, half, s, r, right, left):
-        a, b = pl.ds(0, half), pl.ds(half, half)
-        fa = lax.rem(me + 3, 4)
-        fb = lax.rem(me + 1, 4)
-        ra = send(buf.at[me, a], buf.at[me, a], s.at[0], r.at[0], right)
-        yield
-        lb = send(buf.at[me, b], buf.at[me, b], s.at[1], r.at[1], left)
-        yield
-        ra.wait_recv()
-        fra = send(buf.at[fa, a], buf.at[fa, a], s.at[2], r.at[2], right)
-        lb.wait_recv()
-        flb = send(buf.at[fb, b], buf.at[fb, b], s.at[3], r.at[3], left)
-        yield
-        gone(fra)
-        rb = send(buf.at[me, b], buf.at[me, b], s.at[4], r.at[4], right)
-        gone(flb)
-        la = send(buf.at[me, a], buf.at[me, a], s.at[5], r.at[5], left)
-        yield
-        fra.wait_recv()
-        flb.wait_recv()
-        yield
-        rb.wait_recv()
-        la.wait_recv()
         yield
 
     yring = ring4(ctg, y, 128, ys, yr, yr_dev, yl_dev)
@@ -286,10 +257,9 @@
             copy.wait_recv()
         yield
 
-    spmm(hbuf, hcg.at[x], 0, 4)
-    xring = ring4x(hcg, x, 512, xs, xr, xr_dev, xl_dev)
+    spmm(hbuf, hcg.at[x], 0, 8)
+    xring = ring4(hcg, x, 512, xs, xr, xr_dev, xl_dev)
     next(xring)
-    spmm(hbuf, hcg.at[x], 4, 8)
     next(xring)
     next(yring)
     next(yring)
@@ -307,24 +277,29 @@
             next(reducers[gi])
 
     step(0)
+    step(0)
     next(xring)
-    step(0, 0)
-    next(xring)
-    step(0)
-    next(xring)
-    gram_part(1)
-    step(0, 1)
-    next(sring)
-    step(0, 1)
     next(xring)
     gram_part(2)
     gram_part(3)
-    step(1, 2, 3)
-    step(1, 2, 3)
+    step(0)
+    step(2, 3)
+    next(sring)
+    step(0)
+    step(2, 3)
+    next(xring)
+    gram_part(1)
+    step(2, 3)
+    step(1)
+    step(0)
+    step(2, 3)
+    step(1)
+    step(0)
+    step(2, 3)
+    step(1)
     next(sring)
     next(sring)
-    step(1, 2, 3)
-    step(1)
+    step(2, 3)
 
     def project(p, i):
         total = jnp.zeros((512, 256), F32)
@@ -335,21 +310,21 @@
             )
         return total
 
+    nb_s[0, 1] = project(2, 1).astype(BF)
+    near = [send(nb_s.at[0, 1], nb_r.at[0, 1], fs.at[2], fr.at[2], xr_dev)]
+    nb_s[1, 0] = project(3, 0).astype(BF)
+    near.append(send(nb_s.at[1, 0], nb_r.at[1, 0], fs.at[3], fr.at[3], xl_dev))
+    step(1)
+    racc[0] = project(2, 0)
+    racc[1] = project(3, 1)
+    step(1)
+    step(1)
     opp_s[0] = project(1, 0).astype(BF)
     far_r = send(opp_s.at[0], opp_r.at[0], fs.at[0], fr.at[0], xr_dev)
     opp_s[1] = project(1, 1).astype(BF)
     far_l = send(opp_s.at[1], opp_r.at[1], fs.at[1], fr.at[1], xl_dev)
-    step(2, 3)
     for i in range(2):
         own[i] = hcg[x, pl.ds(i * 512, 512), :].astype(F32) - project(0, i)
-    step(2, 3)
-    step(2, 3)
-    nb_s[0, 1] = project(2, 1).astype(BF)
-    near = [send(nb_s.at[0, 1], nb_r.at[0, 1], fs.at[2], fr.at[2], xr_dev)]
-    nb_s[1, 0] = project(3, 0).astype(BF)
-    near.append(send(nb_s.at[1, 0], nb_r.at[1, 0], fs.at[3], fr.at[3], xl_dev))
-    racc[0] = project(2, 0)
-    racc[1] = project(3, 1)
     far_r.wait_recv()
     nb_s[0, 0] = (racc[0] + opp_r[0].astype(F32)).astype(BF)
     near.append(send(nb_s.at[0, 0], nb_r.at[0, 0], fs.at[4], fr.at[4], xr_dev))

time: 101 us -> 98.8 us (0.978)
  Pallas kernels: 98.6 us -> 96.3 us
    pallas_call x1, Pallas kernels: 98.6 us -> 96.3 us  [body(): pl.pallas_call(kernel, out_shape=jax.ShapeDtypeStruct((1024, 256), F32),...]
where the time goes in v4:
time: 98.8 us; the launch traced here: 98.6 us
  Pallas kernels  96.3 us (97%)
  local copies, waits for them, and re-layouts  2.26 us (2%)
    pallas_call x1, Pallas kernels, body(): pl.pallas_call(kernel, out_shape=jax.ShapeDtypeStruct((1024, 256), F32),...  96.3 us
    unnamed x1, local copies, waits for them, and re-layouts  2.26 us

profile of v4, /device:TPU:1, one launch (start us, length us, event | category | flops | bytes accessed | tf_op | source)
XLA Modules:
  0.0 98.6 jit_solution(17864673605523669545)
XLA Ops:
  0.0 96.3 %block_sparse_residual.1 = f32[1024,256]{1,0:T(8,128)} custom-call(s32[16]{0:T(128)} %sizes.1, s32[16,16]{1,0:T(8,128)} %neigh.1, bf16[2048,256]{1,0:T(8,128)(2,1)} %coeffs.1, bf16[16,8,128,128]{3,2,1,0:T(8,128)(2,1)} %ham.1, bf16[16,8,128,128]{3,2,1,0:T(8,128)(2,1)} %ovl.1), custom_call_target="tpu_custom_call" | custom-call | flops 6442450944 | bytes 12582912 | tf_op jit(solution)/shard_map/block_sparse_residual/pallas_call | solution.py:348
  96.3 2.3 %copy.7 = f32[1024,256]{1,0:T(8,128)} copy(f32[1024,256]{1,0:T(8,128)} %block_sparse_residual.1) | data formatting | bytes 2097152

commit v5 on v4

--- a/solution.py
+++ b/solution.py
@@ -311,26 +311,31 @@
         return total
 
     nb_s[0, 1] = project(2, 1).astype(BF)
-    near = [send(nb_s.at[0, 1], nb_r.at[0, 1], fs.at[2], fr.at[2], xr_dev)]
+    near = [send(nb_s.at[0, 1], nb_r.at[0, 1], fs.at[4], fr.at[4], xr_dev)]
     nb_s[1, 0] = project(3, 0).astype(BF)
-    near.append(send(nb_s.at[1, 0], nb_r.at[1, 0], fs.at[3], fr.at[3], xl_dev))
+    near.append(send(nb_s.at[1, 0], nb_r.at[1, 0], fs.at[5], fr.at[5], xl_dev))
     step(1)
     racc[0] = project(2, 0)
     racc[1] = project(3, 1)
     step(1)
     step(1)
-    opp_s[0] = project(1, 0).astype(BF)
-    far_r = send(opp_s.at[0], opp_r.at[0], fs.at[0], fr.at[0], xr_dev)
-    opp_s[1] = project(1, 1).astype(BF)
-    far_l = send(opp_s.at[1], opp_r.at[1], fs.at[1], fr.at[1], xl_dev)
+    pieces = (pl.ds(0, 256), pl.ds(256, 256))
+    far = []
+    for side, device in ((0, xr_dev), (1, xl_dev)):
+        opp_s[side] = project(1, side).astype(BF)
+        for q, rows in enumerate(pieces):
+            n = 2 * q + side
+            far.append(send(opp_s.at[side, rows], opp_r.at[side, rows], fs.at[n], fr.at[n], device))
     for i in range(2):
         own[i] = hcg[x, pl.ds(i * 512, 512), :].astype(F32) - project(0, i)
-    far_r.wait_recv()
-    nb_s[0, 0] = (racc[0] + opp_r[0].astype(F32)).astype(BF)
-    near.append(send(nb_s.at[0, 0], nb_r.at[0, 0], fs.at[4], fr.at[4], xr_dev))
-    far_l.wait_recv()
-    nb_s[1, 1] = (racc[1] + opp_r[1].astype(F32)).astype(BF)
-    near.append(send(nb_s.at[1, 1], nb_r.at[1, 1], fs.at[5], fr.at[5], xl_dev))
+    for q, rows in enumerate(pieces):
+        for side, device in ((0, xr_dev), (1, xl_dev)):
+            far[2 * side + q].wait_recv()
+            nb_s[side, side, rows] = (racc[side, rows] + opp_r[side, rows].astype(F32)).astype(BF)
+            n = 6 + 2 * q + side
+            near.append(send(
+                nb_s.at[side, side, rows], nb_r.at[side, side, rows], fs.at[n], fr.at[n], device
+            ))
     for copy in near:
         copy.wait_recv()
     for i in range(2):
@@ -382,7 +387,7 @@
             dma((n, 8)), dma((n, 8)),
             dma((n, 8)), dma((n, 8)),
             dma((n, 8)), dma((n, 8)),
-            dma((6,)), dma((6,)),
+            dma((10,)), dma((10,)),
         ],
         compiler_params=pltpu.CompilerParams(
             collective_id=0, has_side_effects=True, vmem_limit_bytes=56 * 2**20

time: 98.8 us -> 96.6 us (0.978)
  Pallas kernels: 96.3 us -> 94.2 us
    pallas_call x1, Pallas kernels: 96.3 us -> 94.2 us  [body(): pl.pallas_call(kernel, out_shape=jax.ShapeDtypeStruct((1024, 256), F32),...]
where the time goes in v5:
time: 96.6 us; the launch traced here: 96.4 us
  Pallas kernels  94.2 us (98%)
  local copies, waits for them, and re-layouts  2.26 us (2%)
    pallas_call x1, Pallas kernels, body(): pl.pallas_call(kernel, out_shape=jax.ShapeDtypeStruct((1024, 256), F32),...  94.2 us
    unnamed x1, local copies, waits for them, and re-layouts  2.26 us

profile of v5, /device:TPU:1, one launch (start us, length us, event | category | flops | bytes accessed | tf_op | source)
XLA Modules:
  0.0 96.4 jit_solution(10671581453151298319)
XLA Ops:
  0.0 94.2 %block_sparse_residual.1 = f32[1024,256]{1,0:T(8,128)} custom-call(s32[16]{0:T(128)} %sizes.1, s32[16,16]{1,0:T(8,128)} %neigh.1, bf16[2048,256]{1,0:T(8,128)(2,1)} %coeffs.1, bf16[16,8,128,128]{3,2,1,0:T(8,128)(2,1)} %ham.1, bf16[16,8,128,128]{3,2,1,0:T(8,128)(2,1)} %ovl.1), custom_call_target="tpu_custom_call" | custom-call | flops 6442450944 | bytes 12582912 | tf_op jit(solution)/shard_map/block_sparse_residual/pallas_call | solution.py:353
  94.2 2.3 %copy.7 = f32[1024,256]{1,0:T(8,128)} copy(f32[1024,256]{1,0:T(8,128)} %block_sparse_residual.1) | data formatting | bytes 2097152

commit v6 on v5

--- a/solution.py
+++ b/solution.py
@@ -71,9 +71,13 @@
 
     pl.semaphore_wait(barrier, 9)
 
-    mine = cbuf.at[pl.ds(16 + l * 8, 8)]
-    to_up = send(mine, cbuf.at[pl.ds(l * 8, 8)], zs.at[0], zr.at[0], up)
-    to_down = send(mine, cbuf.at[pl.ds(32 + l * 8, 8)], zs.at[1], zr.at[1], down)
+    halo = []
+    for q in range(2):
+        mine = cbuf.at[pl.ds(16 + l * 8 + 4 * q, 4)]
+        halo.append((
+            send(mine, cbuf.at[pl.ds(l * 8 + 4 * q, 4)], zs.at[3 * q], zr.at[3 * q], up),
+            send(mine, cbuf.at[pl.ds(32 + l * 8 + 4 * q, 4)], zs.at[3 * q + 1], zr.at[3 * q + 1], down),
+        ))
     give_h = send(
         ham.at[pl.ds((1 - l) * 8, 8)], hbuf.at[:, pl.ds(l * 8, 8)], hs.at[0], hr.at[0], twin
     )
@@ -83,26 +87,37 @@
     def _(i):
         ctg[y, :, pl.ds(pl.multiple_of(i * 128, 128), 128)] = cbuf[16 + l * 8 + i].T
 
-    def ring4(buf, me, half, s, r, right, left):
+    def ring4(buf, me, half, s, r, right, left, pieces=1):
         a, b = pl.ds(0, half), pl.ds(half, half)
         fa = lax.rem(me + 3, 4)
         fb = lax.rem(me + 1, 4)
-        ra = send(buf.at[me, a], buf.at[me, a], s.at[0], r.at[0], right)
-        lb = send(buf.at[me, b], buf.at[me, b], s.at[1], r.at[1], left)
-        yield
-        rb = send(buf.at[me, b], buf.at[me, b], s.at[2], r.at[2], right)
-        la = send(buf.at[me, a], buf.at[me, a], s.at[3], r.at[3], left)
-        yield
-        ra.wait_recv()
-        fra = send(buf.at[fa, a], buf.at[fa, a], s.at[4], r.at[4], right)
-        lb.wait_recv()
-        flb = send(buf.at[fb, b], buf.at[fb, b], s.at[5], r.at[5], left)
-        yield
+        size = half // pieces
+        lows = [pl.ds(q * size, size) for q in range(pieces)]
+        highs = [pl.ds(half + q * size, size) for q in range(pieces)]
+
+        def go(slot, rows, n, device):
+            ref = buf.at[slot, rows]
+            return send(ref, ref, s.at[n], r.at[n], device)
+
+        firsts = [
+            (go(me, lows[q], 4 * q, right), go(me, highs[q], 4 * q + 1, left)) for q in range(pieces)
+        ]
+        yield
+        rb = go(me, b, 4 * pieces, right)
+        la = go(me, a, 4 * pieces + 1, left)
+        yield
+        onward = []
+        for q, (ra, lb) in enumerate(firsts):
+            ra.wait_recv()
+            onward.append(go(fa, lows[q], 4 * q + 2, right))
+            lb.wait_recv()
+            onward.append(go(fb, highs[q], 4 * q + 3, left))
+            yield
         rb.wait_recv()
         la.wait_recv()
         yield
-        fra.wait_recv()
-        flb.wait_recv()
+        for copy in onward:
+            copy.wait_recv()
         yield
 
     yring = ring4(ctg, y, 128, ys, yr, yr_dev, yl_dev)
@@ -118,13 +133,17 @@
         mask_block((1 - l) * 8 + i)
 
     next(yring)
-    to_up.wait_recv()
-    to_down.wait_recv()
     hand = jnp.where(l == 0, 32, 8)
-    take = send(cbuf.at[pl.ds(hand, 8)], cbuf.at[pl.ds(hand, 8)], zs.at[2], zr.at[2], twin)
+    takes = []
+    for q in range(2):
+        for copy in halo[q]:
+            copy.wait_recv()
+        given = cbuf.at[pl.ds(hand + 4 * q, 4)]
+        takes.append(send(given, given, zs.at[3 * q + 2], zr.at[3 * q + 2], twin))
     own_h.wait()
     give_h.wait_recv()
-    take.wait_recv()
+    for copy in takes:
+        copy.wait_recv()
 
     first = z * 16 - 16
 
@@ -258,7 +277,7 @@
         yield
 
     spmm(hbuf, hcg.at[x], 0, 8)
-    xring = ring4(hcg, x, 512, xs, xr, xr_dev, xl_dev)
+    xring = ring4(hcg, x, 512, xs, xr, xr_dev, xl_dev, 2)
     next(xring)
     next(xring)
     next(yring)
@@ -277,6 +296,7 @@
             next(reducers[gi])
 
     step(0)
+    next(xring)
     step(0)
     next(xring)
     next(xring)
@@ -378,10 +398,10 @@
             vmem((2, 512, 256), F32),
             vmem((2, 512, 256), F32),
             dma((3,)),
-            dma((3,)), dma((3,)),
+            dma((6,)), dma((6,)),
             dma((2,)), dma((2,)),
             dma((6,)), dma((6,)),
-            dma((6,)), dma((6,)),
+            dma((10,)), dma((10,)),
             dma((6,)), dma((6,)),
             dma((4,)), dma((4,)),
             dma((n, 8)), dma((n, 8)),

time: 96.6 us -> 96.7 us (level)
  no operation moved by 1% of the time
where the time goes in v6:
time: 96.7 us; the launch traced here: 96.5 us
  Pallas kernels  94.2 us (97%)
  local copies, waits for them, and re-layouts  2.26 us (2%)
    pallas_call x1, Pallas kernels, body(): pl.pallas_call(kernel, out_shape=jax.ShapeDtypeStruct((1024, 256), F32),...  94.2 us
    unnamed x1, local copies, waits for them, and re-layouts  2.26 us

profile of v6, /device:TPU:1, one launch (start us, length us, event | category | flops | bytes accessed | tf_op | source)
XLA Modules:
  0.0 96.5 jit_solution(3500295058423928714)
XLA Ops:
  0.0 94.2 %block_sparse_residual.1 = f32[1024,256]{1,0:T(8,128)} custom-call(s32[16]{0:T(128)} %sizes.1, s32[16,16]{1,0:T(8,128)} %neigh.1, bf16[2048,256]{1,0:T(8,128)(2,1)} %coeffs.1, bf16[16,8,128,128]{3,2,1,0:T(8,128)(2,1)} %ham.1, bf16[16,8,128,128]{3,2,1,0:T(8,128)(2,1)} %ovl.1), custom_call_target="tpu_custom_call" | custom-call | flops 6442450944 | bytes 12582912 | tf_op jit(solution)/shard_map/block_sparse_residual/pallas_call | solution.py:373
  94.3 2.3 %copy.7 = f32[1024,256]{1,0:T(8,128)} copy(f32[1024,256]{1,0:T(8,128)} %block_sparse_residual.1) | data formatting | bytes 2097152
